TPU v7x, 32 devices: a whole 2x2x4 slice. The times are simulated.
32 devices in a mesh: dist: 4 (over x, core), ctr: 8 (over z, y).
Axes of the slice: x: 2, y: 2, z: 4, core: 2. Of those that a mesh axis runs over, the one named last changes fastest.
Arguments:
- three_centre: bfloat16 [1024, 4, 4096], P(('dist', 'ctr')), may hold values from -0.359375 to 0.359375
- occupied_green: bfloat16 [128, 4096], P(('dist', 'ctr')), may hold values from -0.75 to 0.75
- virtual_green: bfloat16 [128, 4096], P(('dist', 'ctr')), may hold values from -0.75 to 0.75
- pair_index: int32 [16, 4], replicated, may hold values from 0 to 7, as said below
- source_slot: int32 [16, 4, 4], replicated, may hold values from -1 to 3, as said below
- occupied_index: int32 [16, 4, 4], replicated, may hold values from 0 to 127, as said below
- virtual_index: int32 [16, 4, 4], replicated, may hold values from 0 to 127, as said below
Outputs:
- density_response: float32 [1024, 256], P(('dist', 'ctr'))
Inputs may be any that keep to these rules, and one draw needn't show every extreme that they name: `pair_index`: the 4 entries of a row are distinct. `source_slot`: for each slot the listed slots are distinct and come first, followed by -1 entries; all slots of one auxiliary atom list the same number of slots, at least 1; in every draw some auxiliary atom lists 4. `occupied_index`: for auxiliary atom p with g = p // 4, every entry lies in g * 32 to g * 32 + 2 * 32 - 1, taken modulo 128. `virtual_index`: for auxiliary atom p with g = p // 4, every entry lies in g * 32 to g * 32 + 2 * 32 - 1, taken modulo 128.
All inputs are finite; a program needn't handle non-finite values.
Results may differ from a plain program's by a relative error of at most 0.004.
Values may be sent and summed in bfloat16 or wider, within the bound.
A program may use at most 64 MiB of HBM per device.

v0:
```python
import jax
import jax.numpy as jnp
from jax import lax
from jax.sharding import PartitionSpec as P

BLK = 64
AUXB = 64
NPR = 8


def shifted(block, axis, distance):
    devices = range(lax.axis_size(axis))
    route = [((i - distance) % len(devices), i) for i in devices]
    return lax.ppermute(block, axis, route)


def shards(
    three_centre,
    occupied_green,
    virtual_green,
    pair_index,
    source_slot,
    occupied_index,
    virtual_index,
):
    row_count = three_centre.shape[0]
    slot_count = three_centre.shape[1]
    ctr_size = lax.axis_size("ctr")
    dist_size = lax.axis_size("dist")
    dist_index = lax.axis_index("dist")
    ctr_index = lax.axis_index("ctr")
    flat_index = dist_index * ctr_size + ctr_index
    atom_index = flat_index * row_count // AUXB
    source_rows = lax.dynamic_index_in_dim(source_slot, atom_index, 0, keepdims=False)
    occ_ids = lax.dynamic_index_in_dim(occupied_index, atom_index, 0, keepdims=False)
    virt_ids = lax.dynamic_index_in_dim(virtual_index, atom_index, 0, keepdims=False)
    occ_own, virt_own = (
        lax.all_gather(occupied_green, "ctr", axis=0, tiled=True),
        lax.all_gather(virtual_green, "ctr", axis=0, tiled=True),
    )
    following = shifted(jnp.stack([occ_own, virt_own]), "dist", -1)
    occ_table = jnp.concatenate([occ_own, following[0]], axis=0)
    virt_table = jnp.concatenate([virt_own, following[1]], axis=0)
    region_base = dist_index * occ_own.shape[0]
    list_total = occ_own.shape[0] * dist_size
    occ_position = jnp.mod(occ_ids - region_base, list_total)
    virt_position = jnp.mod(virt_ids - region_base, list_total)
    tensor_rows = three_centre.reshape(row_count, slot_count, BLK, BLK)
    accumulated = jnp.zeros(tensor_rows.shape, jnp.float32)
    for step in range(source_rows.shape[1]):
        source_col = source_rows[:, step]
        live_mask = (source_col >= 0).astype(jnp.float32)
        picked = jnp.take(tensor_rows, jnp.maximum(source_col, 0), axis=1)
        virt_blocks = jnp.take(virt_table, virt_position[:, step], axis=0).reshape(
            slot_count, BLK, BLK
        )
        product = jnp.einsum(
            "aslv,svz->aslz", picked, virt_blocks, preferred_element_type=jnp.float32
        )
        product = (product * live_mask[None, :, None, None]).astype(jnp.bfloat16)
        occ_blocks = jnp.take(occ_table, occ_position[:, step], axis=0).reshape(
            slot_count, BLK, BLK
        )
        accumulated = accumulated + jnp.einsum(
            "slm,aslz->asmz", occ_blocks, product, preferred_element_type=jnp.float32
        )
    updated = accumulated.astype(jnp.bfloat16).reshape(row_count, slot_count, BLK * BLK)
    upd_region, ten_region = (
        lax.all_to_all(updated, "ctr", split_axis=2, concat_axis=0, tiled=True),
        lax.all_to_all(three_centre, "ctr", split_axis=2, concat_axis=0, tiled=True),
    )
    region_rows = upd_region.shape[0]
    col_count = upd_region.shape[2]
    region_atoms = region_rows // AUXB
    region_pairs = lax.dynamic_slice_in_dim(pair_index, dist_index * region_atoms, region_atoms, 0)
    one_hot = (region_pairs[:, :, None] == jnp.arange(NPR)[None, None, :]).astype(jnp.bfloat16)
    upd_blocks = upd_region.reshape(region_atoms, AUXB, slot_count, col_count)
    ten_blocks = ten_region.reshape(region_atoms, AUXB, slot_count, col_count)
    upd_space = (
        jnp.einsum("psk,pasc->kpac", one_hot, upd_blocks, preferred_element_type=jnp.float32)
        .astype(jnp.bfloat16)
        .reshape(NPR, region_rows, col_count)
    )
    ten_space = (
        jnp.einsum("psk,pasc->kpac", one_hot, ten_blocks, preferred_element_type=jnp.float32)
        .astype(jnp.bfloat16)
        .reshape(NPR, region_rows, col_count)
    )
    return lax.psum_scatter(
        jnp.einsum("kac,kbc->ab", upd_space, ten_space, preferred_element_type=jnp.float32),
        "ctr",
        scatter_dimension=0,
        tiled=True,
    )


def solution(mesh):
    return jax.shard_map(
        shards,
        mesh=mesh,
        in_specs=(
            P(("dist", "ctr"), None, None),
            P(("dist", "ctr"), None),
            P(("dist", "ctr"), None),
            P(),
            P(),
            P(),
            P(),
        ),
        out_specs=P(("dist", "ctr"), None),
        check_vma=False,
    )
```

profile of v0, /device:TPU:0, one launch (start us, length us, event | category | flops | bytes accessed | tf_op | source)
XLA Modules:
  0.0 265.6 jit_solution(9622120785204081876)
XLA Ops:
  6.5 32.9 %all-gather.1 = bf16[8,4,4096]{2,1,0:T(4,128)(2,1)S(1)} all-gather(bf16[1,4,4096]{2,1,0:T(4,128)(2,1)} %bitcast.126), channel_id=1, replica_groups=mesh['dist'=4,'ctr'=8] {'ctr'}, dimensions={0}, use_global_device_ids=true | all-gather | bytes 294912 | tf_op jit(solution)/shard_map/all_gather | solution.py:38
  39.4 30.9 %all-gather = bf16[8,4,4096]{2,1,0:T(4,128)(2,1)S(1)} all-gather(bf16[1,4,4096]{2,1,0:T(4,128)(2,1)} %bitcast.127), channel_id=1, replica_groups=mesh['dist'=4,'ctr'=8] {'ctr'}, dimensions={0}, use_global_device_ids=true | all-gather | bytes 294912 | tf_op jit(solution)/shard_map/all_gather | solution.py:39
  70.5 0.8 pad_maximum_fusion
  71.3 4.8 %copy.40 = bf16[32,4,4096]{0,1,2:T(4,128)(2,1)} copy(bf16[32,4,4096]{2,1,0:T(4,128)(2,1)S(1)} %copy-done.3) | data formatting | bytes 2097152 | tf_op args[0]
  76.2 7.8 %reshape.296 = bf16[8,2,32768]{2,1,0:T(2,128)(2,1)} reshape(bf16[4096,4,32]{2,1,0:T(4,128)(2,1)} %bitcast.120) | data formatting | bytes 2097152
  84.0 5.7 %all-to-all-start.1 = ((bf16[8,2,32768]{2,1,0:T(2,128)(2,1)}), bf16[8,2,32768]{2,1,0:T(2,128)(2,1)}, u32[]{:S(2)}, u32[]{:S(2)}) async-start(bf16[8,2,32768]{2,1,0:T(2,128)(2,1)} %reshape.296), calls=%async_computation.1 | async-start | bytes 2097152 | tf_op jit(solution)/shard_map/all_to_all | solution.py:70
  89.7 0.2 dynamic-slice_reduce_fusion
  89.9 0.2 maximum_reduce_fusion
  90.2 0.2 convert_reduce_fusion
  90.4 0.2 subtract_reduce_fusion
  90.6 0.2 slice_reduce_fusion
  90.8 0.2 subtract_reduce_fusion.1
  91.1 0.2 slice_reduce_fusion.1
  91.4 0.8 reshape.236
  92.2 1.8 reshape.108
  94.3 2.2 gather_fusion.10
  96.4 2.2 gather_fusion.7
  98.6 2.2 gather_fusion.4
  100.8 2.1 gather_fusion.1
  103.0 1.1 slice_bitcast_fusion
  104.0 1.0 pad_maximum_fusion.1
  105.1 0.6 gather_fusion.9
  105.7 0.6 gather_fusion.6
  106.3 0.6 gather_fusion.3
  106.8 0.6 gather_fusion
  107.4 0.6 gather_fusion.11
  108.0 0.6 gather_fusion.8
  108.6 0.6 gather_fusion.5
  109.2 0.6 gather_fusion.2
  109.8 0.1 broadcast_select_fusion.4
  109.9 0.1 reshape.266
  110.0 0.1 broadcast_select_fusion.6
  110.1 0.1 reshape.264
  110.2 0.1 broadcast_select_fusion.2
  110.3 0.1 reshape.268
  110.4 0.1 broadcast_select_fusion
  110.5 0.1 reshape.270
  110.6 0.1 broadcast_select_fusion.5
  110.7 0.1 reshape.110
  110.8 0.1 broadcast_select_fusion.7
  110.9 0.1 reshape.107
  111.1 0.1 broadcast_select_fusion.3
  111.2 0.1 reshape.112
  111.3 0.1 broadcast_select_fusion.1
  111.4 0.1 reshape.114
  111.5 4.7 %fusion.2 = f32[4,32,64,64]{3,2,1,0:T(8,128)} fusion(bf16[4,32,64,64]{3,2,1,0:T(8,128)(2,1)S(1)} %copy-done.2, f32[4]{0:T(128)S(1)} %get-tuple-element.18, pred[4]{0:T(512)(128)(4,1)S(1)} %get-tuple-element.41, bf16[4,64,64]{2,1,0:T(8,128)(2,1)S(1)} %reshape.112, bf16[4,64,64,1]{2,1,0,3:T(8,128)(2,1)S(1)} %reshape.268), kind=kOutput, calls=%fused_computation.19 | convolution fusion | flops 135790592 | bytes 3211284 | tf_op jit(solution)/shard_map/slm,aslz->asmz/dot_general | solution.py:64
  116.2 6.5 %fusion.8 = f32[4,32,64,64]{3,2,1,0:T(8,128)} fusion(bf16[4,32,64,64]{3,2,1,0:T(8,128)(2,1)} %gather_fusion.1, f32[4]{0:T(128)S(1)} %get-tuple-element.16, pred[4]{0:T(512)(128)(4,1)S(1)} %get-tuple-element.47, bf16[4,64,64]{2,1,0:T(8,128)(2,1)S(1)} %reshape.107, bf16[4,64,64,1]{2,1,0,3:T(8,128)(2,1)S(1)} %reshape.264), kind=kOutput, calls=%fused_computation.25 | convolution fusion | flops 135790592 | bytes 3211284 | tf_op jit(solution)/shard_map/slm,aslz->asmz/dot_general | solution.py:64
  122.6 4.7 %fusion.5 = f32[4,32,64,64]{3,2,1,0:T(8,128)} fusion(bf16[4,32,64,64]{3,2,1,0:T(8,128)(2,1)S(1)} %copy-done.1, f32[4]{0:T(128)S(1)} %get-tuple-element.17, pred[4]{0:T(512)(128)(4,1)S(1)} %get-tuple-element.44, bf16[4,64,64]{2,1,0:T(8,128)(2,1)S(1)} %reshape.110, bf16[4,64,64,1]{2,1,0,3:T(8,128)(2,1)S(1)} %reshape.266), kind=kOutput, calls=%fused_computation.22 | convolution fusion | flops 135790592 | bytes 3211284 | tf_op jit(solution)/shard_map/slm,aslz->asmz/dot_general | solution.py:64
  127.4 8.2 %fusion.22 = bf16[32,4,64,64]{2,3,0,1:T(8,128)(2,1)S(1)} fusion(f32[4,32,64,64]{3,2,1,0:T(8,128)} %fusion.2, f32[4,32,64,64]{3,2,1,0:T(8,128)} %fusion.8, f32[4,32,64,64]{3,2,1,0:T(8,128)} %fusion.5, bf16[4,32,64,64]{3,2,1,0:T(8,128)(2,1)} %gather_fusion.10, f32[4]{0:T(128)S(1)} %get-tuple-element.15, pred[4]{0:T(512)(128)(4,1)S(1)} %get-tuple-element.38, ...), kind=kOutput, calls=%fused_computation.41 | convolution fusion | flops 137887744 | bytes 8454164 | tf_op jit(solution)/shard_map/slm,aslz->asmz/dot_general | solution.py:64
  135.6 7.8 %copy.61 = bf16[32,4,64,64]{0,1,3,2:T(4,128)(2,1)} copy(bf16[32,4,64,64]{2,3,0,1:T(8,128)(2,1)S(1)} %fusion.22) | data formatting | bytes 2097152 | tf_op jit(solution)/shard_map/reshape | solution.py:67
  143.4 7.8 %reshape.298 = bf16[8,2,32768]{2,1,0:T(2,128)(2,1)} reshape(bf16[4096,4,32]{2,1,0:T(4,128)(2,1)} %bitcast.117) | data formatting | bytes 2097152
  151.2 6.1 %all-to-all-start = ((bf16[8,2,32768]{2,1,0:T(2,128)(2,1)}), bf16[8,2,32768]{2,1,0:T(2,128)(2,1)S(1)}, u32[]{:S(2)}, u32[]{:S(2)}) async-start(bf16[8,2,32768]{2,1,0:T(2,128)(2,1)} %reshape.298), calls=%async_computation | async-start | bytes 2097152 | tf_op jit(solution)/shard_map/all_to_all | solution.py:69
  157.5 0.1 copy.39
  157.6 7.0 %reshape.297 = bf16[4096,4,32]{2,1,0:T(4,128)(2,1)} reshape(bf16[8,2,32768]{2,1,0:T(2,128)(2,1)} %all-to-all-done.1) | data formatting | bytes 2097152
  164.6 6.1 %copy.41 = bf16[32,4,8,512]{3,1,0,2:T(4,128)(2,1)S(1)} copy(bf16[32,4,8,512]{0,1,3,2:T(4,128)(2,1)} %bitcast.118) | data formatting | bytes 2097152 | tf_op jit(solution)/shard_map/all_to_all | solution.py:70
  170.8 2.2 convolution_convert_fusion
  173.0 10.2 %all-to-all-done = bf16[8,2,32768]{2,1,0:T(2,128)(2,1)S(1)} async-done(((bf16[8,2,32768]{2,1,0:T(2,128)(2,1)}), bf16[8,2,32768]{2,1,0:T(2,128)(2,1)S(1)}, u32[]{:S(2)}, u32[]{:S(2)}) %all-to-all-start) | async-done | bytes 1048608 | tf_op jit(solution)/shard_map/all_to_all | solution.py:69
  183.2 4.5 %reshape.299 = bf16[4096,4,32]{2,1,0:T(4,128)(2,1)} reshape(bf16[8,2,32768]{2,1,0:T(2,128)(2,1)S(1)} %all-to-all-done) | data formatting | bytes 2097152
  187.8 4.7 %copy.62 = bf16[32,4,8,512]{3,2,0,1:T(8,128)(2,1)S(1)} copy(bf16[32,4,8,512]{0,1,3,2:T(4,128)(2,1)} %bitcast.119) | data formatting | bytes 2097152 | tf_op jit(solution)/shard_map/all_to_all | solution.py:69
  192.4 0.8 copy.38
  193.3 1.0 convolution_convert_fusion.1
  194.3 0.5 copy-done.4
  194.9 3.0 %fusion.41 = f32[256,256]{1,0:T(8,128)} fusion(bf16[8,256,512]{2,0,1:T(8,128)(2,1)S(1)} %bitcast.124, bf16[8,256,512]{2,0,1:T(8,128)(2,1)S(1)} %bitcast.125), kind=kOutput, calls=%fused_computation.42 | convolution fusion | flops 536870912 | bytes 4456448 | tf_op jit(solution)/shard_map/kac,kbc->ab/dot_general | solution.py:90
  197.9 60.9 %reduce-scatter.2.cloned.1.call-done = f32[32,256]{1,0:T(8,128)} async-done(((f32[256,256]{1,0:T(8,128)}), f32[32,256]{1,0:T(8,128)}) %reduce-scatter.2.cloned.1.call-update) | async-done | bytes 32784 | tf_op jit(solution)/shard_map/reduce_scatter | solution.py:89
  (50 shorter events, 0.5 us)
Async XLA Ops:
  6.5 83.2 %copy-start = (s32[16,4,4]{0,2,1:T(4,128)S(1)}, s32[16,4,4]{0,2,1:T(4,128)}, u32[]{:S(2)}) copy-start(s32[16,4,4]{0,2,1:T(4,128)} %param.15) | copy-start | bytes 3076
  6.5 64.8 %copy-start.3 = (bf16[32,4,4096]{2,1,0:T(4,128)(2,1)S(1)}, bf16[32,4,4096]{2,1,0:T(4,128)(2,1)}, u32[]{:S(2)}) copy-start(bf16[32,4,4096]{2,1,0:T(4,128)(2,1)} %param.11) | copy-start | bytes 3145732
  71.3 31.6 %collective-permute-start = (bf16[2,32,4096]{2,1,0:T(8,128)(2,1)}, bf16[2,32,4096]{2,1,0:T(8,128)(2,1)}, u32[]{:S(2)}, u32[]{:S(2)}) collective-permute-start(bf16[2,32,4096]{2,1,0:T(8,128)(2,1)} %pad_maximum_fusion), channel_id=1, source_target_pairs={{8,0},{16,8},{24,16},{0,24},{9,1},{17,9},{25,17},{1,25},{10,2},{18... | collective-permute-start | bytes 1572872 | tf_op jit(solution)/shard_map/ppermute | solution.py:14
  84.0 6.3 %copy-start.5 = (s32[16,4,4]{0,2,1:T(4,128)S(1)}, s32[16,4,4]{0,2,1:T(4,128)}, u32[]{:S(2)}) copy-start(s32[16,4,4]{0,2,1:T(4,128)} %param.16) | copy-start | bytes 3076
  84.0 6.8 %copy-start.6 = (s32[16,4,4]{0,2,1:T(4,128)S(1)}, s32[16,4,4]{0,2,1:T(4,128)}, u32[]{:S(2)}) copy-start(s32[16,4,4]{0,2,1:T(4,128)} %param.17) | copy-start | bytes 3076
  84.0 67.2 %all-to-all-start.1 = ((bf16[8,2,32768]{2,1,0:T(2,128)(2,1)}), bf16[8,2,32768]{2,1,0:T(2,128)(2,1)}, u32[]{:S(2)}, u32[]{:S(2)}) async-start(bf16[8,2,32768]{2,1,0:T(2,128)(2,1)} %reshape.296), calls=%async_computation.1 | async-start | bytes 2097152 | tf_op jit(solution)/shard_map/all_to_all | solution.py:70
  105.1 6.4 %copy-start.2 = (bf16[4,32,64,64]{3,2,1,0:T(8,128)(2,1)S(1)}, bf16[4,32,64,64]{3,2,1,0:T(8,128)(2,1)}, u32[]{:S(2)}) copy-start(bf16[4,32,64,64]{3,2,1,0:T(8,128)(2,1)} %gather_fusion.7) | copy-start | bytes 3145732
  116.2 6.5 %copy-start.1 = (bf16[4,32,64,64]{3,2,1,0:T(8,128)(2,1)S(1)}, bf16[4,32,64,64]{3,2,1,0:T(8,128)(2,1)}, u32[]{:S(2)}) copy-start(bf16[4,32,64,64]{3,2,1,0:T(8,128)(2,1)} %gather_fusion.4) | copy-start | bytes 3145732
  151.2 6.2 %copy-start.7 = (s32[16,4]{0,1:T(4,128)S(1)}, s32[16,4]{0,1:T(4,128)}, u32[]{:S(2)}) copy-start(s32[16,4]{0,1:T(4,128)} %param.14) | copy-start | bytes 772
  151.2 32.0 %all-to-all-start = ((bf16[8,2,32768]{2,1,0:T(2,128)(2,1)}), bf16[8,2,32768]{2,1,0:T(2,128)(2,1)S(1)}, u32[]{:S(2)}, u32[]{:S(2)}) async-start(bf16[8,2,32768]{2,1,0:T(2,128)(2,1)} %reshape.298), calls=%async_computation | async-start | bytes 2097152 | tf_op jit(solution)/shard_map/all_to_all | solution.py:69
  157.4 101.4 %reduce-scatter.2.cloned.1.call-start = ((), (), s32[]{:S(2)}) async-start(), calls=%async_computation.3 | async-start | bytes 294912 | tf_op jit(solution)/shard_map/reduce_scatter | solution.py:89
  193.3 1.6 copy-start.4
Sparse Core Ops, SparseCore 0:
  198.0 60.7 reduce-scatter.1
where the time goes:
time: 267 us; the launch traced here: 266 us
  waiting for transfers between devices  71.2 us (27%)
  local copies, waits for them, and re-layouts  71.1 us (27%)
  blocking collectives  63.8 us (24%)
  matrix products  30.3 us (11%)
  between operations  13.8 us (5%)
  starting transfers between devices  11.9 us (4%)
  other arithmetic  3.61 us (1%)
    reduce_scatter x1, waiting for transfers between devices, shards(): lax.psum_scatter(jnp.einsum('kac,kbc->ab', upd_space, ten_space, preferre...  60.9 us
    unnamed x23, local copies, waits for them, and re-layouts  33.5 us
    all_gather x1, blocking collectives, shards(): lax.all_gather(occupied_green, 'ctr', axis=0, tiled=True)  32.9 us
    all_gather x1, blocking collectives, shards(): lax.all_gather(virtual_green, 'ctr', axis=0, tiled=True)  30.9 us
    dot_general x4, matrix products, shards(): jnp.einsum('slm,aslz->asmz', occ_blocks, product, preferred_element_type=...  24.1 us
    all_to_all x1, waiting for transfers between devices, shards(): lax.all_to_all(updated, 'ctr', split_axis=2, concat_axis=0, tiled=True)  10.2 us
    gather x4, local copies, waits for them, and re-layouts, shards(): picked = jnp.take(tensor_rows, jnp.maximum(source_col, 0), axis=1)  8.66 us
    reshape x1, local copies, waits for them, and re-layouts, shards(): accumulated.astype(jnp.bfloat16).reshape(row_count, slot_count, BLK * BLK)  7.84 us
  transfers between devices with their start and end apart: 4, of which 2 were waited for; matrix products, arithmetic and copies ran while one was open for 34% of the time, Pallas kernels for 0%

commit v1 on v0

v1 whole, which is shorter than its diff:
```python
import functools

import jax
import jax.numpy as jnp
from jax import lax
from jax.experimental import pallas as pl
from jax.experimental.pallas import tpu as pltpu
from jax.sharding import PartitionSpec as P

BLK = 64
NPR = 8
LANES = 128
F32 = jnp.float32
BF16 = jnp.bfloat16


def kernel(n, groups, atoms, ids, t_ref, green_ref, out_ref, table, tf, tt, wcat, ocat, usend, urecv, trecv,
           uk, tk, part, precv, g_send, g_recv, t_send, t_recv, u_send, u_recv, p_send, p_recv, own_sem):
    slots, rows, width = t_ref.shape
    chunks = width // LANES
    blocks = green_ref.shape[0]
    cols = width // n
    per = cols // LANES
    dist = lax.axis_index("dist")
    me = lax.axis_index("ctr")
    before = lax.rem(dist + groups - 1, groups)
    after = lax.rem(dist + 1, groups)

    def ahead(k):
        return lax.rem(me + k, n)

    def signal(d, c):
        pl.semaphore_signal(barrier, inc=1, device_id=(d, c), device_id_type=pl.DeviceIdType.MESH)

    def remote(src, dst, send, recv, d, c):
        return pltpu.make_async_remote_copy(
            src_ref=src, dst_ref=dst, send_sem=send, recv_sem=recv, device_id=(d, c),
            device_id_type=pl.DeviceIdType.MESH,
        )

    barrier = pltpu.get_barrier_semaphore()
    for k in range(n):
        if k:
            signal(dist, ahead(k))
        signal(before, ahead(k))
        signal(after, ahead(k))

    row = lax.broadcasted_iota(jnp.int32, (BLK, BLK), 0)
    col = lax.broadcasted_iota(jnp.int32, (BLK, BLK), 1)
    half = BLK // 2
    wanted = jnp.where(row < half, 2 * row, 2 * (row - half) + 1)
    perm = (wanted == col).astype(BF16)
    mine = me * blocks
    for b in range(blocks):
        block = green_ref[b]
        occ = block[:, BLK:]
        turned = lax.dot_general(perm, occ, (((1,), (1,)), ((), ())), preferred_element_type=F32).astype(BF16)
        turned = lax.dot_general(turned, perm, (((1,), (1,)), ((), ())), preferred_element_type=F32).astype(BF16)
        table[mine + b] = jnp.concatenate([block[:, :BLK], turned], axis=1)

    pl.semaphore_wait(barrier, 3 * n - 1)

    green = []
    own = table.at[pl.ds(mine, blocks)]
    there = table.at[pl.ds(n * blocks + mine, blocks)]
    for k in range(n):
        if k:
            green.append(remote(own, own, g_send.at[0, k], g_recv.at[0, k], dist, ahead(k)))
        green.append(remote(own, there, g_send.at[1, k], g_recv.at[1, k], before, ahead(k)))
    for copy in green:
        copy.start()

    def t_part(c):
        return t_ref.at[:, :, pl.ds(pl.multiple_of(c * cols, LANES), cols)]

    tensor = [
        remote(t_part(ahead(k)), trecv.at[me], t_send.at[k], t_recv.at[k], dist, ahead(k)) for k in range(1, n)
    ]
    for copy in tensor:
        copy.start()
    own_t = pltpu.make_async_copy(t_part(me), trecv.at[me], own_sem.at[0])
    own_t.start()

    def turn(s, carry):
        for j in range(chunks):
            tf[j * rows:(j + 1) * rows, :] = t_ref[s, :, j * LANES:(j + 1) * LANES].astype(F32)
        for i in range(rows):
            tt[s, i * chunks:(i + 1) * chunks, :] = tf[pl.ds(i, chunks, stride=rows), :].astype(BF16)
        return carry

    lax.fori_loop(0, slots, turn, 0)

    for copy in green:
        copy.wait()

    size = atoms * slots
    atom = (dist * n + me) * rows // BLK
    total = n * blocks * groups
    base = dist * n * blocks

    def position(value):
        shift = value - base
        return jnp.minimum(jnp.where(shift < 0, shift + total, shift), 2 * n * blocks - 1)

    step_rows = 8 * chunks
    lane = lax.broadcasted_iota(jnp.int32, (half, LANES), 1)

    def update(s, carry):
        at = (atom * slots + s) * slots
        for r in range(slots):
            src = ids[at + r]
            live = jnp.where(src >= 0, 1.0, 0.0).astype(F32)
            src = jnp.maximum(src, 0)
            virt = table[position(ids[2 * size * slots + at + r])].astype(F32)[:, :BLK] * live
            zero = jnp.zeros((BLK, LANES), F32)
            twice = jnp.concatenate([virt, virt], axis=1)
            weight = jnp.concatenate(
                [jnp.concatenate([twice, zero], axis=1), jnp.concatenate([zero, twice], axis=1)], axis=0
            ).astype(BF16)
            ocat[:, r * BLK:(r + 1) * BLK] = table[position(ids[size * slots + at + r])][:, BLK:]
            for h in range(rows // 8):
                got = jnp.dot(
                    tt[src, h * step_rows:(h + 1) * step_rows, :], weight, preferred_element_type=F32
                ).astype(BF16)
                for x in range(8):
                    i = h * 8 + x
                    for e in range(2):
                        wcat[r * BLK + e * half:r * BLK + (e + 1) * half, i * LANES:(i + 1) * LANES] = got[
                            x * chunks:(x + 1) * chunks, e * LANES:(e + 1) * LANES
                        ]
        occ = ocat[...]
        for h in range(rows // 4):
            both = jnp.dot(occ, wcat[:, h * 4 * LANES:(h + 1) * 4 * LANES], preferred_element_type=F32)
            for x in range(4):
                i = h * 4 + x
                piece = both[:, x * LANES:(x + 1) * LANES]
                tf[i * chunks:(i + 1) * chunks, :] = jnp.where(lane < BLK, piece[:half], piece[half:])
        for q in range(chunks):
            usend[s, q // per, :, (q % per) * LANES:(q % per + 1) * LANES] = tf[
                pl.ds(q, rows, stride=chunks), :
            ].astype(BF16)
        for k in range(1, n):
            sent(s, k).start()
        return carry

    def sent(s, k):
        return remote(
            usend.at[s, ahead(k)], urecv.at[me, s], u_send.at[s, k], u_recv.at[s, k], dist, ahead(k)
        )

    lax.fori_loop(0, slots, update, 0)
    own_u = pltpu.make_async_copy(usend.at[:, me], urecv.at[me], own_sem.at[1])
    own_u.start()
    own_t.wait()
    own_u.wait()
    for copy in tensor:
        copy.wait()
    for s in range(slots):
        for k in range(1, n):
            sent(s, k).wait()

    part[...] = jnp.zeros_like(part)
    first = dist * (n * rows // BLK)
    pairs = 3 * size * slots

    def one_pair(pair, carry):
        def gather(p, inner):
            where = pairs + (first + p * rows // BLK) * slots
            slot = jnp.int32(0)
            live = jnp.int32(0)
            for s in range(slots):
                hit = ids[where + s] == pair
                slot = jnp.where(hit, s, slot)
                live = jnp.where(hit, 1, live)
            keep = live.astype(F32)
            at = pl.ds(pl.multiple_of(p * rows, rows), rows)
            uk[at, :] = (urecv[p, slot].astype(F32) * keep).astype(BF16)
            tk[at, :] = (trecv[p, slot].astype(F32) * keep).astype(BF16)
            return inner

        lax.fori_loop(0, n, gather, 0)

        def block(p, inner):
            at = pl.ds(pl.multiple_of(p * 256, 256), 256)
            part[at, :] += lax.dot_general(
                uk[at, :], tk[...], (((1,), (1,)), ((), ())), preferred_element_type=F32
            )
            return inner

        lax.fori_loop(0, n * rows // 256, block, 0)
        return carry

    lax.fori_loop(0, NPR, one_pair, 0)

    def p_part(c):
        return part.at[pl.ds(pl.multiple_of(c * rows, rows), rows)]

    shares = [
        remote(p_part(ahead(k)), precv.at[k], p_send.at[k], p_recv.at[k], dist, ahead(k)) for k in range(1, n)
    ]
    for copy in shares:
        copy.start()
    result = part[pl.ds(pl.multiple_of(me * rows, rows), rows), :]
    for k, copy in enumerate(shares, 1):
        copy.wait()
        result = result + precv[k]
    out_ref[...] = result


def solution(mesh):
    n = mesh.shape["ctr"]
    groups = mesh.shape["dist"]

    def shards(three_centre, occupied_green, virtual_green, pair_index, source_slot, occupied_index, virtual_index):
        rows, slots, width = three_centre.shape
        blocks = occupied_green.shape[0]
        atoms = pair_index.shape[0]
        chunks = width // LANES
        cols = width // n
        tensor = jnp.transpose(three_centre, (1, 0, 2))
        green = jnp.concatenate(
            [virtual_green.reshape(blocks, BLK, BLK), occupied_green.reshape(blocks, BLK, BLK)], axis=2
        )
        ids = jnp.concatenate(
            [x.reshape(-1) for x in (source_slot, occupied_index, virtual_index, pair_index)]
        )
        vmem = pl.BlockSpec(memory_space=pltpu.VMEM)
        dma = pltpu.SemaphoreType.DMA
        return pl.pallas_call(
            functools.partial(kernel, n, groups, atoms),
            out_shape=jax.ShapeDtypeStruct((rows, n * rows), F32),
            in_specs=[pl.BlockSpec(memory_space=pltpu.SMEM), vmem, vmem],
            out_specs=vmem,
            scratch_shapes=[
                pltpu.VMEM((2 * n * blocks, BLK, LANES), BF16),
                pltpu.VMEM((rows * chunks, LANES), F32),
                pltpu.VMEM((slots, rows * chunks, LANES), BF16),
                pltpu.VMEM((slots * BLK, rows * LANES), BF16),
                pltpu.VMEM((BLK, slots * BLK), BF16),
                pltpu.VMEM((slots, n, rows, cols), BF16),
                pltpu.VMEM((n, slots, rows, cols), BF16),
                pltpu.VMEM((n, slots, rows, cols), BF16),
                pltpu.VMEM((n * rows, cols), BF16),
                pltpu.VMEM((n * rows, cols), BF16),
                pltpu.VMEM((n * rows, n * rows), F32),
                pltpu.VMEM((n, rows, n * rows), F32),
                dma((2, n)),
                dma((2, n)),
                dma((n,)),
                dma((n,)),
                dma((slots, n)),
                dma((slots, n)),
                dma((n,)),
                dma((n,)),
                dma((2,)),
            ],
            compiler_params=pltpu.CompilerParams(
                collective_id=0, has_side_effects=True, vmem_limit_bytes=48 * 2**20
            ),
        )(ids, tensor, green)

    return jax.shard_map(
        shards,
        mesh=mesh,
        in_specs=(
            P(("dist", "ctr"), None, None),
            P(("dist", "ctr"), None),
            P(("dist", "ctr"), None),
            P(),
            P(),
            P(),
            P(),
        ),
        out_specs=P(("dist", "ctr"), None),
        check_vma=False,
    )
```

time: 267 us -> 94.6 us (0.35)
  Pallas kernels: 0 us -> 87.5 us
  waiting for transfers between devices: 71.2 us -> 0 us
  local copies, waits for them, and re-layouts: 71.1 us -> 6.5 us
  blocking collectives: 63.8 us -> 0 us
  matrix products: 30.3 us -> 0 us
  between operations: 13.8 us -> 0.05 us
  starting transfers between devices: 11.9 us -> 0 us
  other arithmetic: 3.61 us -> 0.1 us
    pallas_call x0 -> x1, Pallas kernels: none -> 87.5 us  [shards(): pl.pallas_call(functools.partial(kernel, n, groups, atoms), out_shape=jax...]
    all_gather x2 -> x0, blocking collectives: 63.8 us -> none  [the longest x1 32.9 us: shards(): lax.all_gather(occupied_green, 'ctr', axis=0, tiled=True)]
    reduce_scatter x1 -> x0, waiting for transfers between devices: 60.9 us -> none  [shards(): lax.psum_scatter(jnp.einsum('kac,kbc->ab', upd_space, ten_space, preferre...]
    dot_general x7 -> x0, matrix products: 30.3 us -> none  [the longest x4 24.1 us: shards(): jnp.einsum('slm,aslz->asmz', occ_blocks, product, preferred_element_type=...]
    unnamed x23 -> x16, local copies, waits for them, and re-layouts: 33.5 us -> 5.84 us
    gather x12 -> x0, local copies, waits for them, and re-layouts: 13.3 us -> none  [the longest x4 8.66 us: shards(): picked = jnp.take(tensor_rows, jnp.maximum(source_col, 0), axis=1)]
    all_to_all x2 -> x0, starting transfers between devices: 11.8 us -> none  [the longest x1 6.12 us: shards(): lax.all_to_all(updated, 'ctr', split_axis=2, concat_axis=0, tiled=True)]
    all_to_all x3 -> x0, local copies, waits for them, and re-layouts: 11.6 us -> none  [the longest x1 6.13 us: shards(): lax.all_to_all(three_centre, 'ctr', split_axis=2, concat_axis=0, tiled=True)]
  transfers between devices with their start and end apart: 4 -> 0, of which waited for: 2 -> 0; matrix products, arithmetic and copies ran while one was open for 34% -> 0% of each run, Pallas kernels for 0% -> 0%
where the time goes in v1:
time: 94.6 us; the launch traced here: 94.2 us
  Pallas kernels  87.5 us (92%)
  local copies, waits for them, and re-layouts  6.5 us (7%)
    pallas_call x1, Pallas kernels, shards(): pl.pallas_call(functools.partial(kernel, n, groups, atoms), out_shape=jax...  87.5 us
    unnamed x16, local copies, waits for them, and re-layouts  5.84 us

profile of v1, /device:TPU:0, one launch (start us, length us, event | category | flops | bytes accessed | tf_op | source)
XLA Modules:
  0.0 94.2 jit_solution(58865250248340902)
XLA Ops:
  0.0 0.0 copy-start.2
  0.0 0.8 copy.13
  0.8 0.1 reshape.21
  0.9 0.0 copy-done.2
  0.9 0.1 copy.10
  1.0 0.0 copy-start.3
  1.0 0.1 reshape.18
  1.1 0.6 copy-done.3
  1.7 0.1 copy.11
  1.8 0.0 copy-start.4
  1.8 0.1 reshape.19
  1.9 0.6 copy-done.4
  2.5 0.0 copy-start
  2.5 0.1 copy.12
  2.6 0.1 reshape.20
  2.7 0.5 copy-done
  3.2 0.0 copy-start.1
  3.2 0.1 reshape.23
  3.4 0.6 copy-done.1
  4.0 0.1 reshape.22
  4.1 0.1 pad_maximum_fusion.green_ref
  4.2 1.8 %copy.16 = bf16[32,4,4096]{2,0,1:T(8,128)(2,1)S(1)} copy(bf16[32,4,4096]{2,1,0:T(4,128)(2,1)} %param.7) | data formatting | bytes 2097152 | tf_op args[0]
  6.0 87.5 %shard_map.73 = f32[32,256]{1,0:T(8,128)S(1)} custom-call(s32[832]{0:T(1024)S(1)} %pad_add_fusion.ids, bf16[4,32,4096]{2,1,0:T(8,128)(2,1)S(1)} %bitcast.3, bf16[4,64,128]{2,1,0:T(8,128)(2,1)S(1)} %pad_maximum_fusion.green_ref), custom_call_target="tpu_custom_call" | custom-call | tf_op jit(solution)/shard_map/pallas_call | solution.py:229
  93.5 0.6 copy.18
  (1 shorter events, 0.0 us)
Async XLA Ops:
  0.0 0.9 copy-start.2
  1.0 0.7 copy-start.3
  1.8 0.7 copy-start.4
  2.5 0.8 copy-start
  3.2 0.8 copy-start.1

commit v2 on v1

--- a/solution.py
+++ b/solution.py
@@ -15,7 +15,7 @@
 
 
 def kernel(n, groups, atoms, ids, t_ref, green_ref, out_ref, table, tf, tt, wcat, ocat, usend, urecv, trecv,
-           uk, tk, part, precv, g_send, g_recv, t_send, t_recv, u_send, u_recv, p_send, p_recv, own_sem):
+           uk, tk, part, psend, precv, g_send, g_recv, t_send, t_recv, u_send, u_recv, p_send, p_recv, own_sem):
     slots, rows, width = t_ref.shape
     chunks = width // LANES
     blocks = green_ref.shape[0]
@@ -39,11 +39,10 @@
         )
 
     barrier = pltpu.get_barrier_semaphore()
-    for k in range(n):
-        if k:
-            signal(dist, ahead(k))
-        signal(before, ahead(k))
-        signal(after, ahead(k))
+    for k in range(1, n):
+        signal(dist, ahead(k))
+    signal(before, me)
+    signal(after, me)
 
     row = lax.broadcasted_iota(jnp.int32, (BLK, BLK), 0)
     col = lax.broadcasted_iota(jnp.int32, (BLK, BLK), 1)
@@ -58,16 +57,26 @@
         turned = lax.dot_general(turned, perm, (((1,), (1,)), ((), ())), preferred_element_type=F32).astype(BF16)
         table[mine + b] = jnp.concatenate([block[:, :BLK], turned], axis=1)
 
-    pl.semaphore_wait(barrier, 3 * n - 1)
-
-    green = []
-    own = table.at[pl.ds(mine, blocks)]
-    there = table.at[pl.ds(n * blocks + mine, blocks)]
-    for k in range(n):
-        if k:
-            green.append(remote(own, own, g_send.at[0, k], g_recv.at[0, k], dist, ahead(k)))
-        green.append(remote(own, there, g_send.at[1, k], g_recv.at[1, k], before, ahead(k)))
-    for copy in green:
+    pl.semaphore_wait(barrier, n + 1)
+
+    lines = n // 2
+    high, low = me // 2, lax.rem(me, 2)
+    partner = high * 2 + 1 - low
+
+    def line(k):
+        return lax.rem(high + k, lines) * 2
+
+    def at_home(c):
+        return table.at[pl.ds(c * blocks, blocks)]
+
+    def across(c):
+        return table.at[pl.ds((n + c) * blocks, blocks)]
+
+    first_hop = [
+        remote(at_home(me), at_home(me), g_send.at[0, k], g_recv.at[0, k], dist, line(k) + low)
+        for k in range(1, lines)
+    ]
+    for copy in first_hop:
         copy.start()
 
     def t_part(c):
@@ -81,6 +90,16 @@
     own_t = pltpu.make_async_copy(t_part(me), trecv.at[me], own_sem.at[0])
     own_t.start()
 
+    second_hop, third_hop = [], []
+    for k in range(lines):
+        if k:
+            first_hop[k - 1].wait_recv()
+        c = line(lines - k) + low
+        second_hop.append(remote(at_home(c), at_home(c), g_send.at[1, k], g_recv.at[1, k], dist, partner))
+        second_hop[-1].start()
+        third_hop.append(remote(at_home(c), across(c), g_send.at[2, k], g_recv.at[2, k], before, me))
+        third_hop[-1].start()
+
     def turn(s, carry):
         for j in range(chunks):
             tf[j * rows:(j + 1) * rows, :] = t_ref[s, :, j * LANES:(j + 1) * LANES].astype(F32)
@@ -90,8 +109,15 @@
 
     lax.fori_loop(0, slots, turn, 0)
 
-    for copy in green:
+    for k in range(lines):
+        second_hop[k].wait_recv()
+        c = line(lines - k) + 1 - low
+        third_hop.append(remote(at_home(c), across(c), g_send.at[3, k], g_recv.at[3, k], before, me))
+        third_hop[-1].start()
+    for copy in third_hop:
         copy.wait()
+    for copy in first_hop + second_hop:
+        copy.wait_send()
 
     size = atoms * slots
     atom = (dist * n + me) * rows // BLK
@@ -192,8 +218,10 @@
 
     lax.fori_loop(0, NPR, one_pair, 0)
 
+    psend[...] = part[...].astype(BF16)
+
     def p_part(c):
-        return part.at[pl.ds(pl.multiple_of(c * rows, rows), rows)]
+        return psend.at[pl.ds(pl.multiple_of(c * rows, rows), rows)]
 
     shares = [
         remote(p_part(ahead(k)), precv.at[k], p_send.at[k], p_recv.at[k], dist, ahead(k)) for k in range(1, n)
@@ -203,7 +231,7 @@
     result = part[pl.ds(pl.multiple_of(me * rows, rows), rows), :]
     for k, copy in enumerate(shares, 1):
         copy.wait()
-        result = result + precv[k]
+        result = result + precv[k].astype(F32)
     out_ref[...] = result
 
 
@@ -243,9 +271,10 @@
                 pltpu.VMEM((n * rows, cols), BF16),
                 pltpu.VMEM((n * rows, cols), BF16),
                 pltpu.VMEM((n * rows, n * rows), F32),
-                pltpu.VMEM((n, rows, n * rows), F32),
-                dma((2, n)),
-                dma((2, n)),
+                pltpu.VMEM((n * rows, n * rows), BF16),
+                pltpu.VMEM((n, rows, n * rows), BF16),
+                dma((4, n // 2)),
+                dma((4, n // 2)),
                 dma((n,)),
                 dma((n,)),
                 dma((slots, n)),

time: 94.6 us -> 75.6 us (0.80)
  Pallas kernels: 87.5 us -> 68.6 us
    pallas_call x1, Pallas kernels: 87.5 us -> 68.6 us  [shards(): pl.pallas_call(functools.partial(kernel, n, groups, atoms), out_shape=jax...]
where the time goes in v2:
time: 75.6 us; the launch traced here: 75.2 us
  Pallas kernels  68.6 us (91%)
  local copies, waits for them, and re-layouts  6.5 us (9%)
    pallas_call x1, Pallas kernels, shards(): pl.pallas_call(functools.partial(kernel, n, groups, atoms), out_shape=jax...  68.6 us
    unnamed x16, local copies, waits for them, and re-layouts  5.84 us

profile of v2, /device:TPU:0, one launch (start us, length us, event | category | flops | bytes accessed | tf_op | source)
XLA Modules:
  0.0 75.2 jit_solution(13391148012613949664)
XLA Ops:
  0.0 0.0 copy-start.2
  0.0 0.8 %copy.13 = s32[16,4]{1,0:T(8,128)S(1)} copy(s32[16,4]{0,1:T(4,128)} %param.10) | data formatting | bytes 512 | tf_op args[3]
  0.8 0.1 reshape.21
  0.9 0.0 copy-done.2
  0.9 0.1 copy.10
  1.0 0.0 copy-start.3
  1.0 0.1 reshape.18
  1.1 0.6 copy-done.3
  1.7 0.1 copy.11
  1.8 0.0 copy-start.4
  1.8 0.1 reshape.19
  1.9 0.6 copy-done.4
  2.5 0.0 copy-start
  2.5 0.1 copy.12
  2.6 0.1 reshape.20
  2.7 0.5 copy-done
  3.2 0.0 copy-start.1
  3.2 0.1 reshape.23
  3.4 0.6 copy-done.1
  4.0 0.1 reshape.22
  4.1 0.1 pad_maximum_fusion.green_ref
  4.2 1.8 %copy.16 = bf16[32,4,4096]{2,0,1:T(8,128)(2,1)S(1)} copy(bf16[32,4,4096]{2,1,0:T(4,128)(2,1)} %param.7) | data formatting | bytes 2097152 | tf_op args[0]
  6.0 68.6 %shard_map.73 = f32[32,256]{1,0:T(8,128)S(1)} custom-call(s32[832]{0:T(1024)S(1)} %pad_add_fusion.ids, bf16[4,32,4096]{2,1,0:T(8,128)(2,1)S(1)} %bitcast.3, bf16[4,64,128]{2,1,0:T(8,128)(2,1)S(1)} %pad_maximum_fusion.green_ref), custom_call_target="tpu_custom_call" | custom-call | tf_op jit(solution)/shard_map/pallas_call | solution.py:257
  74.6 0.6 copy.18
  (1 shorter events, 0.0 us)
Async XLA Ops:
  0.0 0.9 %copy-start.2 = (s32[16,4,4]{0,2,1:T(4,128)S(1)}, s32[16,4,4]{0,2,1:T(4,128)}, u32[]{:S(2)}) copy-start(s32[16,4,4]{0,2,1:T(4,128)} %param.11) | copy-start | bytes 3076
  1.0 0.7 copy-start.3
  1.8 0.7 copy-start.4
  2.5 0.8 %copy-start = (bf16[4,4096]{1,0:T(4,128)(2,1)S(1)}, bf16[4,4096]{1,0:T(4,128)(2,1)}, u32[]{:S(2)}) copy-start(bf16[4,4096]{1,0:T(4,128)(2,1)} %param.8) | copy-start | bytes 98308
  3.2 0.8 %copy-start.1 = (bf16[4,4096]{1,0:T(4,128)(2,1)S(1)}, bf16[4,4096]{1,0:T(4,128)(2,1)}, u32[]{:S(2)}) copy-start(bf16[4,4096]{1,0:T(4,128)(2,1)} %param.9) | copy-start | bytes 98308

commit v3 on v2

--- a/solution.py
+++ b/solution.py
@@ -19,7 +19,8 @@
     slots, rows, width = t_ref.shape
     chunks = width // LANES
     blocks = green_ref.shape[0]
-    cols = width // n
+    team = n // 2
+    cols = width // team
     per = cols // LANES
     dist = lax.axis_index("dist")
     me = lax.axis_index("ctr")
@@ -28,6 +29,12 @@
 
     def ahead(k):
         return lax.rem(me + k, n)
+
+    lead = me // team * team
+    place = lax.rem(me, team)
+
+    def mate(k):
+        return lax.rem(place + k, team)
 
     def signal(d, c):
         pl.semaphore_signal(barrier, inc=1, device_id=(d, c), device_id_type=pl.DeviceIdType.MESH)
@@ -80,7 +87,7 @@
         copy.start()
 
     def t_part(c):
-        return t_ref.at[:, :, pl.ds(pl.multiple_of(c * cols, LANES), cols)]
+        return t_ref.at[:, :, pl.ds(pl.multiple_of(lax.rem(c, team) * cols, LANES), cols)]
 
     tensor = [
         remote(t_part(ahead(k)), trecv.at[me], t_send.at[k], t_recv.at[k], dist, ahead(k)) for k in range(1, n)
@@ -165,24 +172,24 @@
             usend[s, q // per, :, (q % per) * LANES:(q % per + 1) * LANES] = tf[
                 pl.ds(q, rows, stride=chunks), :
             ].astype(BF16)
-        for k in range(1, n):
+        for k in range(1, team):
             sent(s, k).start()
         return carry
 
     def sent(s, k):
         return remote(
-            usend.at[s, ahead(k)], urecv.at[me, s], u_send.at[s, k], u_recv.at[s, k], dist, ahead(k)
+            usend.at[s, mate(k)], urecv.at[place, s], u_send.at[s, k], u_recv.at[s, k], dist, lead + mate(k)
         )
 
     lax.fori_loop(0, slots, update, 0)
-    own_u = pltpu.make_async_copy(usend.at[:, me], urecv.at[me], own_sem.at[1])
+    own_u = pltpu.make_async_copy(usend.at[:, place], urecv.at[place], own_sem.at[1])
     own_u.start()
     own_t.wait()
     own_u.wait()
     for copy in tensor:
         copy.wait()
     for s in range(slots):
-        for k in range(1, n):
+        for k in range(1, team):
             sent(s, k).wait()
 
     part[...] = jnp.zeros_like(part)
@@ -190,30 +197,36 @@
     pairs = 3 * size * slots
 
     def one_pair(pair, carry):
-        def gather(p, inner):
-            where = pairs + (first + p * rows // BLK) * slots
+        def pick(dst, src, owner, p):
+            where = pairs + (first + owner * rows // BLK) * slots
             slot = jnp.int32(0)
             live = jnp.int32(0)
             for s in range(slots):
                 hit = ids[where + s] == pair
                 slot = jnp.where(hit, s, slot)
                 live = jnp.where(hit, 1, live)
-            keep = live.astype(F32)
             at = pl.ds(pl.multiple_of(p * rows, rows), rows)
-            uk[at, :] = (urecv[p, slot].astype(F32) * keep).astype(BF16)
-            tk[at, :] = (trecv[p, slot].astype(F32) * keep).astype(BF16)
+            dst[at, :] = (src[p, slot].astype(F32) * live.astype(F32)).astype(BF16)
+
+        def gather_t(p, inner):
+            pick(tk, trecv, p, p)
             return inner
 
-        lax.fori_loop(0, n, gather, 0)
+        def gather_u(p, inner):
+            pick(uk, urecv, lead + p, p)
+            return inner
+
+        lax.fori_loop(0, n, gather_t, 0)
+        lax.fori_loop(0, team, gather_u, 0)
 
         def block(p, inner):
-            at = pl.ds(pl.multiple_of(p * 256, 256), 256)
+            at = pl.ds(pl.multiple_of(p * LANES, LANES), LANES)
             part[at, :] += lax.dot_general(
                 uk[at, :], tk[...], (((1,), (1,)), ((), ())), preferred_element_type=F32
             )
             return inner
 
-        lax.fori_loop(0, n * rows // 256, block, 0)
+        lax.fori_loop(0, team * rows // LANES, block, 0)
         return carry
 
     lax.fori_loop(0, NPR, one_pair, 0)
@@ -224,11 +237,12 @@
         return psend.at[pl.ds(pl.multiple_of(c * rows, rows), rows)]
 
     shares = [
-        remote(p_part(ahead(k)), precv.at[k], p_send.at[k], p_recv.at[k], dist, ahead(k)) for k in range(1, n)
+        remote(p_part(mate(k)), precv.at[k], p_send.at[k], p_recv.at[k], dist, lead + mate(k))
+        for k in range(1, team)
     ]
     for copy in shares:
         copy.start()
-    result = part[pl.ds(pl.multiple_of(me * rows, rows), rows), :]
+    result = part[pl.ds(pl.multiple_of(place * rows, rows), rows), :]
     for k, copy in enumerate(shares, 1):
         copy.wait()
         result = result + precv[k].astype(F32)
@@ -244,7 +258,8 @@
         blocks = occupied_green.shape[0]
         atoms = pair_index.shape[0]
         chunks = width // LANES
-        cols = width // n
+        team = n // 2
+        cols = width // team
         tensor = jnp.transpose(three_centre, (1, 0, 2))
         green = jnp.concatenate(
             [virtual_green.reshape(blocks, BLK, BLK), occupied_green.reshape(blocks, BLK, BLK)], axis=2
@@ -265,22 +280,22 @@
                 pltpu.VMEM((slots, rows * chunks, LANES), BF16),
                 pltpu.VMEM((slots * BLK, rows * LANES), BF16),
                 pltpu.VMEM((BLK, slots * BLK), BF16),
-                pltpu.VMEM((slots, n, rows, cols), BF16),
+                pltpu.VMEM((slots, team, rows, cols), BF16),
+                pltpu.VMEM((team, slots, rows, cols), BF16),
                 pltpu.VMEM((n, slots, rows, cols), BF16),
-                pltpu.VMEM((n, slots, rows, cols), BF16),
+                pltpu.VMEM((team * rows, cols), BF16),
                 pltpu.VMEM((n * rows, cols), BF16),
-                pltpu.VMEM((n * rows, cols), BF16),
-                pltpu.VMEM((n * rows, n * rows), F32),
-                pltpu.VMEM((n * rows, n * rows), BF16),
-                pltpu.VMEM((n, rows, n * rows), BF16),
+                pltpu.VMEM((team * rows, n * rows), F32),
+                pltpu.VMEM((team * rows, n * rows), BF16),
+                pltpu.VMEM((team, rows, n * rows), BF16),
                 dma((4, n // 2)),
                 dma((4, n // 2)),
                 dma((n,)),
                 dma((n,)),
-                dma((slots, n)),
-                dma((slots, n)),
-                dma((n,)),
-                dma((n,)),
+                dma((slots, team)),
+                dma((slots, team)),
+                dma((team,)),
+                dma((team,)),
                 dma((2,)),
             ],
             compiler_params=pltpu.CompilerParams(

time: 75.6 us -> 83.4 us (1.10)
  the two profiles are of different devices: /device:TPU:0 before, /device:TPU:18 now
where the time goes in v3:
time: 83.4 us; the launch traced here: 83 us
  Pallas kernels  76.4 us (92%)
  local copies, waits for them, and re-layouts  6.5 us (8%)
    pallas_call x1, Pallas kernels, shards(): pl.pallas_call(functools.partial(kernel, n, groups, atoms), out_shape=jax...  76.4 us
    unnamed x16, local copies, waits for them, and re-layouts  5.84 us

profile of v3, /device:TPU:18, one launch (start us, length us, event | category | flops | bytes accessed | tf_op | source)
XLA Modules:
  0.0 83.0 jit_solution(4944026124149767322)
XLA Ops:
  0.0 0.0 copy-start.2
  0.0 0.8 copy.13
  0.8 0.1 reshape.21
  0.9 0.0 copy-done.2
  0.9 0.1 copy.10
  1.0 0.0 copy-start.3
  1.0 0.1 reshape.18
  1.1 0.6 copy-done.3
  1.7 0.1 copy.11
  1.8 0.0 copy-start.4
  1.8 0.1 reshape.19
  1.9 0.6 copy-done.4
  2.5 0.0 copy-start
  2.5 0.1 copy.12
  2.6 0.1 reshape.20
  2.7 0.5 copy-done
  3.2 0.0 copy-start.1
  3.2 0.1 reshape.23
  3.4 0.6 copy-done.1
  4.0 0.1 reshape.22
  4.1 0.1 pad_maximum_fusion.green_ref
  4.2 1.8 %copy.16 = bf16[32,4,4096]{2,0,1:T(8,128)(2,1)S(1)} copy(bf16[32,4,4096]{2,1,0:T(4,128)(2,1)} %param.7) | data formatting | bytes 2097152 | tf_op args[0]
  6.0 76.4 %shard_map.73 = f32[32,256]{1,0:T(8,128)S(1)} custom-call(s32[832]{0:T(1024)S(1)} %pad_add_fusion.ids, bf16[4,32,4096]{2,1,0:T(8,128)(2,1)S(1)} %bitcast.3, bf16[4,64,128]{2,1,0:T(8,128)(2,1)S(1)} %pad_maximum_fusion.green_ref), custom_call_target="tpu_custom_call" | custom-call | tf_op jit(solution)/shard_map/pallas_call | solution.py:272
  82.4 0.6 copy.18
  (1 shorter events, 0.0 us)
Async XLA Ops:
  0.0 0.9 %copy-start.2 = (s32[16,4,4]{0,2,1:T(4,128)S(1)}, s32[16,4,4]{0,2,1:T(4,128)}, u32[]{:S(2)}) copy-start(s32[16,4,4]{0,2,1:T(4,128)} %param.11) | copy-start | bytes 3076
  1.0 0.7 copy-start.3
  1.8 0.7 copy-start.4
  2.5 0.8 copy-start
  3.2 0.8 copy-start.1

commit v4 on v2

--- a/solution.py
+++ b/solution.py
@@ -25,6 +25,8 @@
     me = lax.axis_index("ctr")
     before = lax.rem(dist + groups - 1, groups)
     after = lax.rem(dist + 1, groups)
+
+    far_first = sorted(range(1, n), key=lambda k: -min(k, n - k))
 
     def ahead(k):
         return lax.rem(me + k, n)
@@ -83,7 +85,7 @@
         return t_ref.at[:, :, pl.ds(pl.multiple_of(c * cols, LANES), cols)]
 
     tensor = [
-        remote(t_part(ahead(k)), trecv.at[me], t_send.at[k], t_recv.at[k], dist, ahead(k)) for k in range(1, n)
+        remote(t_part(ahead(k)), trecv.at[me], t_send.at[k], t_recv.at[k], dist, ahead(k)) for k in far_first
     ]
     for copy in tensor:
         copy.start()
@@ -165,7 +167,7 @@
             usend[s, q // per, :, (q % per) * LANES:(q % per + 1) * LANES] = tf[
                 pl.ds(q, rows, stride=chunks), :
             ].astype(BF16)
-        for k in range(1, n):
+        for k in far_first:
             sent(s, k).start()
         return carry
 
@@ -178,30 +180,43 @@
     own_u = pltpu.make_async_copy(usend.at[:, me], urecv.at[me], own_sem.at[1])
     own_u.start()
     own_t.wait()
-    own_u.wait()
     for copy in tensor:
         copy.wait()
+
+    first = dist * (n * rows // BLK)
+    pairs = 3 * size * slots
+
+    def pick(src, pair, p):
+        where = pairs + (first + p * rows // BLK) * slots
+        slot = jnp.int32(0)
+        live = jnp.int32(0)
+        for s in range(slots):
+            hit = ids[where + s] == pair
+            slot = jnp.where(hit, s, slot)
+            live = jnp.where(hit, 1, live)
+        return (src[p, slot].astype(F32) * live.astype(F32)).astype(BF16)
+
+    def at_rows(p):
+        return pl.ds(pl.multiple_of(p * rows, rows), rows)
+
+    def tensor_pair(pair, carry):
+        def gather(p, inner):
+            tk[pair, at_rows(p), :] = pick(trecv, pair, p)
+            return inner
+
+        return lax.fori_loop(0, n, gather, carry)
+
+    lax.fori_loop(0, NPR, tensor_pair, 0)
+    part[...] = jnp.zeros_like(part)
+
+    own_u.wait()
     for s in range(slots):
         for k in range(1, n):
             sent(s, k).wait()
 
-    part[...] = jnp.zeros_like(part)
-    first = dist * (n * rows // BLK)
-    pairs = 3 * size * slots
-
     def one_pair(pair, carry):
         def gather(p, inner):
-            where = pairs + (first + p * rows // BLK) * slots
-            slot = jnp.int32(0)
-            live = jnp.int32(0)
-            for s in range(slots):
-                hit = ids[where + s] == pair
-                slot = jnp.where(hit, s, slot)
-                live = jnp.where(hit, 1, live)
-            keep = live.astype(F32)
-            at = pl.ds(pl.multiple_of(p * rows, rows), rows)
-            uk[at, :] = (urecv[p, slot].astype(F32) * keep).astype(BF16)
-            tk[at, :] = (trecv[p, slot].astype(F32) * keep).astype(BF16)
+            uk[at_rows(p), :] = pick(urecv, pair, p)
             return inner
 
         lax.fori_loop(0, n, gather, 0)
@@ -209,7 +224,7 @@
         def block(p, inner):
             at = pl.ds(pl.multiple_of(p * 256, 256), 256)
             part[at, :] += lax.dot_general(
-                uk[at, :], tk[...], (((1,), (1,)), ((), ())), preferred_element_type=F32
+                uk[at, :], tk[pair], (((1,), (1,)), ((), ())), preferred_element_type=F32
             )
             return inner
 
@@ -224,12 +239,12 @@
         return psend.at[pl.ds(pl.multiple_of(c * rows, rows), rows)]
 
     shares = [
-        remote(p_part(ahead(k)), precv.at[k], p_send.at[k], p_recv.at[k], dist, ahead(k)) for k in range(1, n)
+        remote(p_part(ahead(k)), precv.at[k], p_send.at[k], p_recv.at[k], dist, ahead(k)) for k in far_first
     ]
     for copy in shares:
         copy.start()
     result = part[pl.ds(pl.multiple_of(me * rows, rows), rows), :]
-    for k, copy in enumerate(shares, 1):
+    for k, copy in zip(far_first, shares):
         copy.wait()
         result = result + precv[k].astype(F32)
     out_ref[...] = result
@@ -269,7 +284,7 @@
                 pltpu.VMEM((n, slots, rows, cols), BF16),
                 pltpu.VMEM((n, slots, rows, cols), BF16),
                 pltpu.VMEM((n * rows, cols), BF16),
-                pltpu.VMEM((n * rows, cols), BF16),
+                pltpu.VMEM((NPR, n * rows, cols), BF16),
                 pltpu.VMEM((n * rows, n * rows), F32),
                 pltpu.VMEM((n * rows, n * rows), BF16),
                 pltpu.VMEM((n, rows, n * rows), BF16),

time: 75.6 us -> 75.6 us (level)
  no operation moved by 1% of the time
where the time goes in v4:
time: 75.6 us; the launch traced here: 75.1 us
  Pallas kernels  68.5 us (91%)
  local copies, waits for them, and re-layouts  6.5 us (9%)
    pallas_call x1, Pallas kernels, shards(): pl.pallas_call(functools.partial(kernel, n, groups, atoms), out_shape=jax...  68.5 us
    unnamed x16, local copies, waits for them, and re-layouts  5.84 us

profile of v4, /device:TPU:0, one launch (start us, length us, event | category | flops | bytes accessed | tf_op | source)
XLA Modules:
  0.0 75.1 jit_solution(17887974699836524837)
XLA Ops:
  0.0 0.0 copy-start.2
  0.0 0.8 %copy.13 = s32[16,4]{1,0:T(8,128)S(1)} copy(s32[16,4]{0,1:T(4,128)} %param.10) | data formatting | bytes 512 | tf_op args[3]
  0.8 0.1 reshape.21
  0.9 0.0 copy-done.2
  0.9 0.1 copy.10
  1.0 0.0 copy-start.3
  1.0 0.1 reshape.18
  1.1 0.6 copy-done.3
  1.7 0.1 copy.11
  1.8 0.0 copy-start.4
  1.8 0.1 reshape.19
  1.9 0.6 copy-done.4
  2.5 0.0 copy-start
  2.5 0.1 copy.12
  2.6 0.1 reshape.20
  2.7 0.5 copy-done
  3.2 0.0 copy-start.1
  3.2 0.1 reshape.23
  3.4 0.6 copy-done.1
  4.0 0.1 reshape.22
  4.1 0.1 pad_maximum_fusion.green_ref
  4.2 1.8 %copy.16 = bf16[32,4,4096]{2,0,1:T(8,128)(2,1)S(1)} copy(bf16[32,4,4096]{2,1,0:T(4,128)(2,1)} %param.7) | data formatting | bytes 2097152 | tf_op args[0]
  6.0 68.5 %shard_map.73 = f32[32,256]{1,0:T(8,128)S(1)} custom-call(s32[832]{0:T(1024)S(1)} %pad_add_fusion.ids, bf16[4,32,4096]{2,1,0:T(8,128)(2,1)S(1)} %bitcast.3, bf16[4,64,128]{2,1,0:T(8,128)(2,1)S(1)} %pad_maximum_fusion.green_ref), custom_call_target="tpu_custom_call" | custom-call | tf_op jit(solution)/shard_map/pallas_call | solution.py:272
  74.5 0.6 copy.18
  (1 shorter events, 0.0 us)
Async XLA Ops:
  0.0 0.9 %copy-start.2 = (s32[16,4,4]{0,2,1:T(4,128)S(1)}, s32[16,4,4]{0,2,1:T(4,128)}, u32[]{:S(2)}) copy-start(s32[16,4,4]{0,2,1:T(4,128)} %param.11) | copy-start | bytes 3076
  1.0 0.7 copy-start.3
  1.8 0.7 copy-start.4
  2.5 0.8 %copy-start = (bf16[4,4096]{1,0:T(4,128)(2,1)S(1)}, bf16[4,4096]{1,0:T(4,128)(2,1)}, u32[]{:S(2)}) copy-start(bf16[4,4096]{1,0:T(4,128)(2,1)} %param.8) | copy-start | bytes 98308
  3.2 0.8 %copy-start.1 = (bf16[4,4096]{1,0:T(4,128)(2,1)S(1)}, bf16[4,4096]{1,0:T(4,128)(2,1)}, u32[]{:S(2)}) copy-start(bf16[4,4096]{1,0:T(4,128)(2,1)} %param.9) | copy-start | bytes 98308

commit v5 on v4

--- a/solution.py
+++ b/solution.py
@@ -199,15 +199,17 @@
     def at_rows(p):
         return pl.ds(pl.multiple_of(p * rows, rows), rows)
 
+    def at_cols(pair):
+        return pl.ds(pl.multiple_of(pair * cols, LANES), cols)
+
     def tensor_pair(pair, carry):
         def gather(p, inner):
-            tk[pair, at_rows(p), :] = pick(trecv, pair, p)
+            tk[at_rows(p), at_cols(pair)] = pick(trecv, pair, p)
             return inner
 
         return lax.fori_loop(0, n, gather, carry)
 
     lax.fori_loop(0, NPR, tensor_pair, 0)
-    part[...] = jnp.zeros_like(part)
 
     own_u.wait()
     for s in range(slots):
@@ -216,24 +218,23 @@
 
     def one_pair(pair, carry):
         def gather(p, inner):
-            uk[at_rows(p), :] = pick(urecv, pair, p)
+            uk[at_rows(p), at_cols(pair)] = pick(urecv, pair, p)
             return inner
 
         lax.fori_loop(0, n, gather, 0)
 
-        def block(p, inner):
-            at = pl.ds(pl.multiple_of(p * 256, 256), 256)
-            part[at, :] += lax.dot_general(
-                uk[at, :], tk[pair], (((1,), (1,)), ((), ())), preferred_element_type=F32
-            )
-            return inner
-
-        lax.fori_loop(0, n * rows // 256, block, 0)
         return carry
 
     lax.fori_loop(0, NPR, one_pair, 0)
 
-    psend[...] = part[...].astype(BF16)
+    def block(p, carry):
+        at = pl.ds(pl.multiple_of(p * 256, 256), 256)
+        total = lax.dot_general(uk[at, :], tk[...], (((1,), (1,)), ((), ())), preferred_element_type=F32)
+        part[at, :] = total
+        psend[at, :] = total.astype(BF16)
+        return carry
+
+    lax.fori_loop(0, n * rows // 256, block, 0)
 
     def p_part(c):
         return psend.at[pl.ds(pl.multiple_of(c * rows, rows), rows)]
@@ -283,8 +284,8 @@
                 pltpu.VMEM((slots, n, rows, cols), BF16),
                 pltpu.VMEM((n, slots, rows, cols), BF16),
                 pltpu.VMEM((n, slots, rows, cols), BF16),
-                pltpu.VMEM((n * rows, cols), BF16),
-                pltpu.VMEM((NPR, n * rows, cols), BF16),
+                pltpu.VMEM((n * rows, NPR * cols), BF16),
+                pltpu.VMEM((n * rows, NPR * cols), BF16),
                 pltpu.VMEM((n * rows, n * rows), F32),
                 pltpu.VMEM((n * rows, n * rows), BF16),
                 pltpu.VMEM((n, rows, n * rows), BF16),

time: 75.6 us -> 74.3 us (0.983)
  Pallas kernels: 68.5 us -> 67.3 us
    pallas_call x1, Pallas kernels: 68.5 us -> 67.3 us  [shards(): pl.pallas_call(functools.partial(kernel, n, groups, atoms), out_shape=jax...]
where the time goes in v5:
time: 74.3 us; the launch traced here: 73.9 us
  Pallas kernels  67.3 us (91%)
  local copies, waits for them, and re-layouts  6.5 us (9%)
    pallas_call x1, Pallas kernels, shards(): pl.pallas_call(functools.partial(kernel, n, groups, atoms), out_shape=jax...  67.3 us
    unnamed x16, local copies, waits for them, and re-layouts  5.84 us

profile of v5, /device:TPU:0, one launch (start us, length us, event | category | flops | bytes accessed | tf_op | source)
XLA Modules:
  0.0 73.9 jit_solution(16488145015346317567)
XLA Ops:
  0.0 0.0 copy-start.2
  0.0 0.8 %copy.13 = s32[16,4]{1,0:T(8,128)S(1)} copy(s32[16,4]{0,1:T(4,128)} %param.10) | data formatting | bytes 512 | tf_op args[3]
  0.8 0.1 reshape.21
  0.9 0.0 copy-done.2
  0.9 0.1 copy.10
  1.0 0.0 copy-start.3
  1.0 0.1 reshape.18
  1.1 0.6 copy-done.3
  1.7 0.1 copy.11
  1.8 0.0 copy-start.4
  1.8 0.1 reshape.19
  1.9 0.6 copy-done.4
  2.5 0.0 copy-start
  2.5 0.1 copy.12
  2.6 0.1 reshape.20
  2.7 0.5 copy-done
  3.2 0.0 copy-start.1
  3.2 0.1 reshape.23
  3.4 0.6 copy-done.1
  4.0 0.1 reshape.22
  4.1 0.1 pad_maximum_fusion.green_ref
  4.2 1.8 %copy.16 = bf16[32,4,4096]{2,0,1:T(8,128)(2,1)S(1)} copy(bf16[32,4,4096]{2,1,0:T(4,128)(2,1)} %param.7) | data formatting | bytes 2097152 | tf_op args[0]
  6.0 67.3 %shard_map.73 = f32[32,256]{1,0:T(8,128)S(1)} custom-call(s32[832]{0:T(1024)S(1)} %pad_add_fusion.ids, bf16[4,32,4096]{2,1,0:T(8,128)(2,1)S(1)} %bitcast.3, bf16[4,64,128]{2,1,0:T(8,128)(2,1)S(1)} %pad_maximum_fusion.green_ref), custom_call_target="tpu_custom_call" | custom-call | tf_op jit(solution)/shard_map/pallas_call | solution.py:273
  73.3 0.6 copy.18
  (1 shorter events, 0.0 us)
Async XLA Ops:
  0.0 0.9 %copy-start.2 = (s32[16,4,4]{0,2,1:T(4,128)S(1)}, s32[16,4,4]{0,2,1:T(4,128)}, u32[]{:S(2)}) copy-start(s32[16,4,4]{0,2,1:T(4,128)} %param.11) | copy-start | bytes 3076
  1.0 0.7 copy-start.3
  1.8 0.7 copy-start.4
  2.5 0.8 %copy-start = (bf16[4,4096]{1,0:T(4,128)(2,1)S(1)}, bf16[4,4096]{1,0:T(4,128)(2,1)}, u32[]{:S(2)}) copy-start(bf16[4,4096]{1,0:T(4,128)(2,1)} %param.8) | copy-start | bytes 98308
  3.2 0.8 %copy-start.1 = (bf16[4,4096]{1,0:T(4,128)(2,1)S(1)}, bf16[4,4096]{1,0:T(4,128)(2,1)}, u32[]{:S(2)}) copy-start(bf16[4,4096]{1,0:T(4,128)(2,1)} %param.9) | copy-start | bytes 98308

commit v6 on v5

--- a/solution.py
+++ b/solution.py
@@ -211,21 +211,25 @@
 
     lax.fori_loop(0, NPR, tensor_pair, 0)
 
+    def updated_pairs(p):
+        where = pairs + (first + p * rows // BLK) * slots
+
+        def one_pair(pair, carry):
+            chosen = jnp.zeros((rows, cols), F32)
+            for s in range(slots):
+                hit = jnp.where(ids[where + s] == pair, 1.0, 0.0).astype(F32)
+                chosen = chosen + urecv[p, s].astype(F32) * hit
+            uk[at_rows(p), at_cols(pair)] = chosen.astype(BF16)
+            return carry
+
+        lax.fori_loop(0, NPR, one_pair, 0)
+
     own_u.wait()
-    for s in range(slots):
-        for k in range(1, n):
+    updated_pairs(me)
+    for k in far_first[::-1]:
+        for s in range(slots):
             sent(s, k).wait()
-
-    def one_pair(pair, carry):
-        def gather(p, inner):
-            uk[at_rows(p), at_cols(pair)] = pick(urecv, pair, p)
-            return inner
-
-        lax.fori_loop(0, n, gather, 0)
-
-        return carry
-
-    lax.fori_loop(0, NPR, one_pair, 0)
+        updated_pairs(lax.rem(me - k + n, n))
 
     def block(p, carry):
         at = pl.ds(pl.multiple_of(p * 256, 256), 256)

time: 74.3 us -> 73.5 us (0.989)
  Pallas kernels: 67.3 us -> 66.4 us
    pallas_call x1, Pallas kernels: 67.3 us -> 66.4 us  [shards(): pl.pallas_call(functools.partial(kernel, n, groups, atoms), out_shape=jax...]
where the time goes in v6:
time: 73.5 us; the launch traced here: 73.1 us
  Pallas kernels  66.4 us (90%)
  local copies, waits for them, and re-layouts  6.5 us (9%)
    pallas_call x1, Pallas kernels, shards(): pl.pallas_call(functools.partial(kernel, n, groups, atoms), out_shape=jax...  66.4 us
    unnamed x16, local copies, waits for them, and re-layouts  5.84 us

profile of v6, /device:TPU:0, one launch (start us, length us, event | category | flops | bytes accessed | tf_op | source)
XLA Modules:
  0.0 73.1 jit_solution(17776435055086892882)
XLA Ops:
  0.0 0.0 copy-start.2
  0.0 0.8 %copy.13 = s32[16,4]{1,0:T(8,128)S(1)} copy(s32[16,4]{0,1:T(4,128)} %param.10) | data formatting | bytes 512 | tf_op args[3]
  0.8 0.1 reshape.21
  0.9 0.0 copy-done.2
  0.9 0.1 copy.10
  1.0 0.0 copy-start.3
  1.0 0.1 reshape.18
  1.1 0.6 copy-done.3
  1.7 0.1 copy.11
  1.8 0.0 copy-start.4
  1.8 0.1 reshape.19
  1.9 0.6 copy-done.4
  2.5 0.0 copy-start
  2.5 0.1 copy.12
  2.6 0.1 reshape.20
  2.7 0.5 copy-done
  3.2 0.0 copy-start.1
  3.2 0.1 reshape.23
  3.4 0.6 copy-done.1
  4.0 0.1 reshape.22
  4.1 0.1 pad_maximum_fusion.green_ref
  4.2 1.8 %copy.16 = bf16[32,4,4096]{2,0,1:T(8,128)(2,1)S(1)} copy(bf16[32,4,4096]{2,1,0:T(4,128)(2,1)} %param.7) | data formatting | bytes 2097152 | tf_op args[0]
  6.0 66.4 %shard_map.73 = f32[32,256]{1,0:T(8,128)S(1)} custom-call(s32[832]{0:T(1024)S(1)} %pad_add_fusion.ids, bf16[4,32,4096]{2,1,0:T(8,128)(2,1)S(1)} %bitcast.3, bf16[4,64,128]{2,1,0:T(8,128)(2,1)S(1)} %pad_maximum_fusion.green_ref), custom_call_target="tpu_custom_call" | custom-call | tf_op jit(solution)/shard_map/pallas_call | solution.py:277
  72.5 0.6 copy.18
  (1 shorter events, 0.0 us)
Async XLA Ops:
  0.0 0.9 %copy-start.2 = (s32[16,4,4]{0,2,1:T(4,128)S(1)}, s32[16,4,4]{0,2,1:T(4,128)}, u32[]{:S(2)}) copy-start(s32[16,4,4]{0,2,1:T(4,128)} %param.11) | copy-start | bytes 3076
  1.0 0.7 copy-start.3
  1.8 0.7 copy-start.4
  2.5 0.8 %copy-start = (bf16[4,4096]{1,0:T(4,128)(2,1)S(1)}, bf16[4,4096]{1,0:T(4,128)(2,1)}, u32[]{:S(2)}) copy-start(bf16[4,4096]{1,0:T(4,128)(2,1)} %param.8) | copy-start | bytes 98308
  3.2 0.8 %copy-start.1 = (bf16[4,4096]{1,0:T(4,128)(2,1)S(1)}, bf16[4,4096]{1,0:T(4,128)(2,1)}, u32[]{:S(2)}) copy-start(bf16[4,4096]{1,0:T(4,128)(2,1)} %param.9) | copy-start | bytes 98308

commit v7 on v6

--- a/solution.py
+++ b/solution.py
@@ -18,7 +18,7 @@
            uk, tk, part, psend, precv, g_send, g_recv, t_send, t_recv, u_send, u_recv, p_send, p_recv, own_sem):
     slots, rows, width = t_ref.shape
     chunks = width // LANES
-    blocks = green_ref.shape[0]
+    blocks = green_ref.shape[0] // 2
     cols = width // n
     per = cols // LANES
     dist = lax.axis_index("dist")
@@ -53,11 +53,10 @@
     perm = (wanted == col).astype(BF16)
     mine = me * blocks
     for b in range(blocks):
-        block = green_ref[b]
-        occ = block[:, BLK:]
+        occ = green_ref[blocks + b]
         turned = lax.dot_general(perm, occ, (((1,), (1,)), ((), ())), preferred_element_type=F32).astype(BF16)
         turned = lax.dot_general(turned, perm, (((1,), (1,)), ((), ())), preferred_element_type=F32).astype(BF16)
-        table[mine + b] = jnp.concatenate([block[:, :BLK], turned], axis=1)
+        table[mine + b] = jnp.concatenate([green_ref[b], turned], axis=1)
 
     pl.semaphore_wait(barrier, n + 1)
 
@@ -266,9 +265,7 @@
         chunks = width // LANES
         cols = width // n
         tensor = jnp.transpose(three_centre, (1, 0, 2))
-        green = jnp.concatenate(
-            [virtual_green.reshape(blocks, BLK, BLK), occupied_green.reshape(blocks, BLK, BLK)], axis=2
-        )
+        green = jnp.concatenate([virtual_green, occupied_green], axis=0).reshape(2 * blocks, BLK, BLK)
         ids = jnp.concatenate(
             [x.reshape(-1) for x in (source_slot, occupied_index, virtual_index, pair_index)]
         )

time: 73.5 us -> 72.7 us (0.989)
  no operation moved by 1% of the time
where the time goes in v7:
time: 72.7 us; the launch traced here: 72.3 us
  Pallas kernels  66.4 us (91%)
  local copies, waits for them, and re-layouts  5.81 us (8%)
    pallas_call x1, Pallas kernels, shards(): pl.pallas_call(functools.partial(kernel, n, groups, atoms), out_shape=jax...  66.4 us
    unnamed x16, local copies, waits for them, and re-layouts  5.22 us

profile of v7, /device:TPU:0, one launch (start us, length us, event | category | flops | bytes accessed | tf_op | source)
XLA Modules:
  0.0 72.3 jit_solution(16890440151395129961)
XLA Ops:
  0.0 0.0 copy-start.2
  0.0 0.8 %copy.13 = s32[16,4]{1,0:T(8,128)S(1)} copy(s32[16,4]{0,1:T(4,128)} %param.10) | data formatting | bytes 512 | tf_op args[3]
  0.8 0.1 reshape.18
  0.9 0.0 copy-done.2
  0.9 0.1 copy.10
  1.0 0.0 copy-start.3
  1.0 0.1 reshape.15
  1.1 0.6 copy-done.3
  1.7 0.1 copy.11
  1.8 0.0 copy-start.4
  1.8 0.1 reshape.16
  1.9 0.6 copy-done.4
  2.5 0.0 copy-start
  2.5 0.0 copy-start.1
  2.5 0.1 copy.12
  2.6 0.1 reshape.17
  2.7 0.5 copy-done
  3.2 0.0 copy-done.1
  3.3 0.2 reshape.19.green_ref
  3.5 1.8 %copy.16 = bf16[32,4,4096]{2,0,1:T(8,128)(2,1)S(1)} copy(bf16[32,4,4096]{2,1,0:T(4,128)(2,1)} %param.7) | data formatting | bytes 2097152 | tf_op args[0]
  5.3 66.4 %shard_map.73 = f32[32,256]{1,0:T(8,128)S(1)} custom-call(s32[832]{0:T(1024)S(1)} %pad_add_fusion.ids, bf16[4,32,4096]{2,1,0:T(8,128)(2,1)S(1)} %bitcast.3, bf16[8,64,64]{2,1,0:T(8,128)(2,1)S(1)} %reshape.19.green_ref), custom_call_target="tpu_custom_call" | custom-call | tf_op jit(solution)/shard_map/pallas_call | solution.py:274
  71.7 0.6 copy.18
  (2 shorter events, 0.0 us)
Async XLA Ops:
  0.0 0.9 %copy-start.2 = (s32[16,4,4]{0,2,1:T(4,128)S(1)}, s32[16,4,4]{0,2,1:T(4,128)}, u32[]{:S(2)}) copy-start(s32[16,4,4]{0,2,1:T(4,128)} %param.11) | copy-start | bytes 3076
  1.0 0.7 copy-start.3
  1.8 0.7 copy-start.4
  2.5 0.8 %copy-start = (bf16[4,4096]{1,0:T(4,128)(2,1)S(1)}, bf16[4,4096]{1,0:T(4,128)(2,1)}, u32[]{:S(2)}) copy-start(bf16[4,4096]{1,0:T(4,128)(2,1)} %param.8) | copy-start | bytes 98308
  2.5 0.8 %copy-start.1 = (bf16[4,4096]{1,0:T(4,128)(2,1)S(1)}, bf16[4,4096]{1,0:T(4,128)(2,1)}, u32[]{:S(2)}) copy-start(bf16[4,4096]{1,0:T(4,128)(2,1)} %param.9) | copy-start | bytes 98308
